TPU v7x, 32 devices: a whole 2x2x4 slice. The times are simulated.
32 devices in a mesh: grp: 2 (over y), col: 8 (over z, x), row: 2 (over core).
Axes of the slice: x: 2, y: 2, z: 4, core: 2. Of those that a mesh axis runs over, the one named last changes fastest.
Arguments:
- pair_block: float32 [4, 16, 1152, 128], P('grp', 'row', 'col'), parts along dimension 0, may hold values from -260 to 260
- query_single: bfloat16 [4, 16, 768], P('grp', 'row'), parts along dimension 0, may hold values from -70 to 70
- key_single: bfloat16 [2304, 768], P(('grp', 'col')), parts along dimension 0, may hold values from -70 to 70
- query_chain: int32 [4, 16], P('grp', 'row'), parts along dimension 0, may hold values from 0 to 23
- key_chain: int32 [2304], P(('grp', 'col')), parts along dimension 0, may hold values from 0 to 23, never falling along the last dimension, each value on 1 to 144 neighbouring positions
- query_mask: int32 [4, 16], P('grp', 'row'), parts along dimension 0, may hold values 0 or 1
- key_mask: int32 [2304], P(('grp', 'col')), parts along dimension 0, may hold values 0 or 1
- timestep: int32 [2], P('grp'), parts along dimension 0, may hold values from 0 to 49
- time_table: bfloat16 [50, 768], replicated, may hold values from -6 to 6
- norm_gain: float32 [768], replicated, may hold values from 0.1 to 1.9
- left_proj: bfloat16 [768, 8], replicated, may hold values from -0.21875 to 0.21875
- right_proj: bfloat16 [768, 8], replicated, may hold values from -0.21875 to 0.21875
- outer_proj: bfloat16 [64, 128], replicated, may hold values from -0.75 to 0.75
- bias_proj: float32 [128, 12], replicated, may hold values from -0.75 to 0.75
- chain_weight: float32 [12], replicated, may hold values from -2 to 2
- query_proj: bfloat16 [768, 1536], P(None, 'col'), may hold values from -0.21875 to 0.21875
- kv_proj: bfloat16 [768, 1536], P(None, 'row'), may hold values from -0.21875 to 0.21875
- out_proj: bfloat16 [768, 768], replicated, may hold values from -0.75 to 0.75
Outputs:
- new_pair: float32 [4, 16, 1152, 128], P('grp', 'row', 'col'), parts along dimension 0
- single_update: bfloat16 [4, 16, 768], P('grp', 'row'), parts along dimension 0
There are 2 independent parts, one for each index of `grp`. A program takes and returns all parts, laid end to end along the dimension named above; an argument that names none is the same for every part. Nothing has to cross between parts.
Inputs may be any that keep to these rules, and one draw needn't show every extreme that they name: `key_chain`: never falling along the residues; each of the 24 chains holds at least one residue.
All inputs are finite; a program needn't handle non-finite values. No bound on the sum of `query_mask` or of `key_mask` on one device may be relied on, other than what follows from the above.
Results may differ from a plain program's by a relative error of at most 0.0082.
Values may be sent and summed in bfloat16 or wider, within the bound.
A program may use at most 64 MiB of HBM per device.

v0:
```python
import math

import jax
import jax.numpy as jnp
from jax import lax
from jax.sharding import PartitionSpec as P

EPSILON = 1e-05
HIGHEST = lax.Precision.HIGHEST


def combined_all(part, axis, combine):
    gathered = jax.tree.map(lambda a: lax.all_gather(a, axis), part)

    def take(source):
        return jax.tree.map(lambda a: lax.dynamic_index_in_dim(a, source, 0, False), gathered)

    return lax.fori_loop(
        1, lax.axis_size(axis), lambda source, state: combine(state, take(source)), take(0)
    )


def normalize(features, norm_gain):
    average = jnp.mean(features, axis=-1, keepdims=True)
    centred = features - average
    spread = jnp.mean(centred * centred, axis=-1, keepdims=True)
    return (centred * lax.rsqrt(spread + EPSILON) * norm_gain).astype(jnp.bfloat16)


def flat_dot(left, right):
    flat_left = left.reshape(-1, left.shape[-1])
    product = jnp.dot(flat_left, right, preferred_element_type=jnp.float32)
    return product.reshape(left.shape[:-1] + (right.shape[-1],))


def combine_parts(former, latter):
    peak_former, total_former, summed_former = former
    peak_latter, total_latter, summed_latter = latter
    peak_joint = jnp.maximum(peak_former, peak_latter)
    scale_former = jnp.exp(peak_former - peak_joint)
    scale_latter = jnp.exp(peak_latter - peak_joint)
    head_width = summed_former.shape[-1] // peak_joint.shape[-1]
    total_joint = total_former * scale_former + total_latter * scale_latter
    summed_joint = summed_former * jnp.repeat(
        scale_former, head_width, axis=-1
    ) + summed_latter * jnp.repeat(scale_latter, head_width, axis=-1)
    return (peak_joint, total_joint, summed_joint)


def local_parts(query_heads, key_heads, value_heads, logit_bias):
    scores = (
        jnp.einsum("srhd,jhd->srhj", query_heads, key_heads, preferred_element_type=jnp.float32)
        * (1.0 / math.sqrt(query_heads.shape[-1]))
        + logit_bias
    )
    maxima = jnp.max(scores, axis=-1)
    exponent = jnp.exp(scores - maxima[..., None])
    totals = jnp.sum(exponent, axis=-1)
    summed = jnp.einsum(
        "srhj,jhd->srhd",
        exponent.astype(jnp.bfloat16),
        value_heads,
        preferred_element_type=jnp.float32,
    )
    return (maxima, totals, summed.reshape(summed.shape[0], summed.shape[1], -1))


def finish(partials, gate_factor, out_proj, heads):
    maxima, totals, summed = combined_all(partials, "col", combine_parts)
    head_width = summed.shape[-1] // heads
    attended = (summed / jnp.repeat(totals, head_width, axis=-1) * gate_factor).astype(jnp.bfloat16)
    return flat_dot(attended, out_proj).astype(jnp.bfloat16)


def on_device(
    pair_block,
    query_single,
    key_single,
    query_chain,
    key_chain,
    query_mask,
    key_mask,
    timestep,
    time_table,
    norm_gain,
    left_proj,
    right_proj,
    outer_proj,
    bias_proj,
    chain_weight,
    query_proj,
    kv_proj,
    out_proj,
):
    step_count = time_table.shape[0]
    picked = jnp.arange(step_count, dtype=jnp.int32) == timestep[0]
    time_row = jnp.sum(
        jnp.where(picked[:, None], time_table.astype(jnp.float32), jnp.float32(0.0)), axis=0
    )
    query_norm = normalize(
        query_single.astype(jnp.float32) + query_mask[:, :, None].astype(jnp.float32) * time_row,
        norm_gain,
    )
    key_norm = normalize(
        key_single.astype(jnp.float32) + key_mask[:, None].astype(jnp.float32) * time_row, norm_gain
    )
    query_part = flat_dot(query_norm, query_proj).astype(jnp.bfloat16)
    query_gate = lax.all_gather(query_part, "col", axis=2, tiled=True)
    half_projected = jnp.dot(key_norm, kv_proj, preferred_element_type=jnp.float32).astype(
        jnp.bfloat16
    )
    keys_values = lax.all_gather(half_projected, "row", axis=1, tiled=True)
    rank = left_proj.shape[1]
    channels = outer_proj.shape[1]
    left_factor = flat_dot(query_norm, left_proj)
    right_factor = jnp.dot(key_norm, right_proj, preferred_element_type=jnp.float32)
    mixer = jnp.einsum(
        "sra,abc->srbc",
        left_factor,
        outer_proj.astype(jnp.float32).reshape(rank, rank, channels),
        precision=HIGHEST,
    )
    new_pair = pair_block + jnp.einsum("jb,srbc->srjc", right_factor, mixer, precision=HIGHEST)
    differ = (query_chain[:, :, None] != key_chain[None, None, :]).astype(jnp.float32)
    logit_bias = (
        jnp.einsum("srjc,ch->srhj", new_pair, bias_proj, precision=HIGHEST)
        + chain_weight[None, None, :, None] * differ[:, :, None, :]
    )
    heads = chain_weight.shape[0]
    model_width = query_norm.shape[-1]
    head_size = model_width // heads
    slab_count = query_gate.shape[0]
    slab_rows = query_gate.shape[1]
    key_count = keys_values.shape[0]
    query_heads = query_gate[:, :, :model_width].reshape(slab_count, slab_rows, heads, head_size)
    gate_factor = jax.nn.sigmoid(query_gate[:, :, model_width:].astype(jnp.float32))
    key_heads = keys_values[:, :model_width].reshape(key_count, heads, head_size)
    value_heads = keys_values[:, model_width:].reshape(key_count, heads, head_size)
    single_update = finish(
        local_parts(query_heads, key_heads, value_heads, logit_bias), gate_factor, out_proj, heads
    )
    return (new_pair, single_update)


def solution(mesh):
    return jax.shard_map(
        on_device,
        mesh=mesh,
        in_specs=(
            P("grp", "row", "col", None),
            P("grp", "row", None),
            P(("grp", "col"), None),
            P("grp", "row"),
            P(("grp", "col")),
            P("grp", "row"),
            P(("grp", "col")),
            P("grp"),
            P(),
            P(),
            P(),
            P(),
            P(),
            P(),
            P(),
            P(None, "col"),
            P(None, "row"),
            P(),
        ),
        out_specs=(P("grp", "row", "col", None), P("grp", "row", None)),
        check_vma=False,
    )
```

profile of v0, /device:TPU:0, one launch (start us, length us, event | category | flops | bytes accessed | tf_op | source)
XLA Modules:
  0.0 153.0 jit_solution(936284778297747066)
XLA Ops:
  1.5 0.7 convert_element_type.50
  2.1 0.7 convert_element_type.54
  2.8 1.0 select_reduce_fusion
  3.8 1.1 fusion.13
  5.0 1.2 multiply_reduce_fusion
  6.2 0.9 fusion.23
  7.1 0.9 multiply_reduce_fusion.1
  8.0 1.2 convolution_convert_fusion.1
  9.2 1.0 convolution_bitcast_fusion.4
  10.2 0.9 convolution_bitcast_fusion.3
  11.2 0.8 fusion.25
  12.0 0.1 copy.34
  12.1 0.4 convolution_convert_fusion
  12.6 2.2 %all_gather.21 = bf16[144,1536]{1,0:T(8,128)(2,1)S(1)} all-gather(bf16[144,768]{1,0:T(8,128)(2,1)S(1)} %convolution_convert_fusion), channel_id=1, replica_groups=mesh['grp'=2,'col'=8,'row'=2] {'row'}, dimensions={1}, use_global_device_ids=true | all-gather | bytes 663552 | tf_op jit(solution)/shard_map/all_gather | solution.py:112
  14.8 0.9 copy.40
  15.7 0.2 copy.33
  15.9 34.0 %all_gather.22 = bf16[2,8,1536]{1,0,2:T(2,128)(2,1)S(1)} all-gather(bf16[2,8,192]{1,0,2:T(2,128)(2,1)S(1)} %copy.34), channel_id=1, replica_groups=mesh['grp'=2,'col'=8,'row'=2] {'col'}, dimensions={2}, use_global_device_ids=true | all-gather | bytes 55296 | tf_op jit(solution)/shard_map/all_gather | solution.py:108
  49.9 0.5 fusion.33
  50.4 0.9 copy.36
  51.3 0.3 copy.48
  51.6 2.0 %fusion.3 = f32[2,8,144,128]{3,2,1,0:T(8,128)S(1)} fusion(f32[2,8,144,128]{3,2,1,0:T(8,128)S(1)} %copy-done.2, f32[144,8,1,1]{0,1,3,2:T(8,128)} %convolution_bitcast_fusion.3, f32[2,8,8,128]{3,1,2,0:T(8,128)} %fusion.25), kind=kOutput, calls=%fused_computation.9 | convolution fusion | flops 28606464 | bytes 2429440 | tf_op jit(solution)/shard_map/jb,srbc->srjc/dot_general | solution.py:123
  53.7 1.9 %fusion.29 = f32[2,8,144,12]{2,3,1,0:T(8,128)S(1)} fusion(f32[2,8,144,128]{3,2,1,0:T(8,128)S(1)} %fusion.3, f32[128,12]{0,1:T(8,128)S(1)} %copy-done.8), kind=kOutput, calls=%fused_computation.50 | convolution fusion | flops 42467328 | bytes 1296384 | tf_op jit(solution)/shard_map/srjc,ch->srhj/dot_general | solution.py:126
  55.6 0.3 fusion.35
  55.9 0.3 convolution_bitcast_fusion.2
  56.2 0.2 fusion.16
  56.7 30.5 %all-gather.1 = f32[16,8,12]{2,1,0:T(8,128)S(1)} all-gather(f32[2,8,12]{2,1,0:T(8,128)S(1)} %copy.39), channel_id=3, replica_groups=mesh['grp'=2,'col'=8,'row'=2] {'col'}, dimensions={0}, use_global_device_ids=true | all-gather | bytes 6912 | tf_op jit(solution)/shard_map/all_gather | solution.py:13
  87.2 30.5 %all-gather = f32[16,8,12]{2,1,0:T(8,128)S(1)} all-gather(f32[2,8,12]{2,1,0:T(8,128)S(1)} %copy.38), channel_id=2, replica_groups=mesh['grp'=2,'col'=8,'row'=2] {'col'}, dimensions={0}, use_global_device_ids=true | all-gather | bytes 6912 | tf_op jit(solution)/shard_map/all_gather | solution.py:13
  117.7 31.1 %all_gather.27 = f32[8,2,8,768]{3,2,1,0:T(8,128)S(1)} all-gather(f32[1,2,8,768]{3,2,1,0:T(8,128)S(1)} %all_gather_reshape.3), channel_id=1, replica_groups=mesh['grp'=2,'col'=8,'row'=2] {'col'}, dimensions={0}, use_global_device_ids=true | all-gather | bytes 442368 | tf_op jit(solution)/shard_map/all_gather | solution.py:13
  148.8 3.2 %while.19 = (s32[]{:T(128)}, f32[2,8,12]{2,1,0:T(8,128)S(1)}, f32[2,8,12]{2,1,0:T(8,128)S(1)}, f32[2,8,768]{2,1,0:T(8,128)S(1)}, f32[8,2,8,12]{3,2,1,0:T(8,128)S...) while((s32[]{:T(128)}, f32[2,8,12]{2,1,0:T(8,128)S(1)}, ...), condition=%wide.region_8.9_spmd, body=%wide.region_7.8_spmd.sunk | while | flops 38021 | bytes 548495 | solution.py:18
  148.9 0.1 reshape.117
  149.0 0.1 broadcast_in_dim.59
  149.1 0.1 reshape.118
  149.3 0.1 broadcast_in_dim.58
  149.4 0.1 reshape.117
  149.5 0.1 broadcast_in_dim.59
  149.6 0.1 reshape.118
  149.8 0.1 reshape.117
  150.0 0.1 reshape.118
  150.3 0.1 reshape.117
  150.5 0.1 reshape.118
  150.7 0.1 reshape.117
  150.9 0.1 reshape.118
  151.2 0.1 reshape.117
  151.4 0.1 reshape.118
  151.6 0.1 reshape.117
  151.8 0.1 reshape.118
  152.1 0.1 reshape.97
  152.2 0.9 fusion.9
  (68 shorter events, 1.9 us)
Async XLA Ops:
  0.6 11.5 %copy-start = (bf16[768,768]{1,0:T(8,128)(2,1)S(1)}, bf16[768,768]{1,0:T(8,128)(2,1)}, u32[]{:S(2)}) copy-start(bf16[768,768]{1,0:T(8,128)(2,1)} %param.36) | copy-start | bytes 3538948
  0.6 9.6 %copy-start.13 = (f32[768]{0:T(1024)S(1)}, f32[768]{0:T(1024)}, u32[]{:S(2)}) copy-start(f32[768]{0:T(1024)} %param.29) | copy-start | bytes 9220
  0.7 9.5 %copy-start.4 = (bf16[144,768]{1,0:T(8,128)(2,1)S(1)}, bf16[144,768]{1,0:T(8,128)(2,1)}, u32[]{:S(2)}) copy-start(bf16[144,768]{1,0:T(8,128)(2,1)} %param.22) | copy-start | bytes 663556
  0.7 10.5 %copy-start.7 = (bf16[64,128]{1,0:T(8,128)(2,1)S(1)}, bf16[64,128]{1,0:T(8,128)(2,1)}, u32[]{:S(2)}) copy-start(bf16[64,128]{1,0:T(8,128)(2,1)} %param.32) | copy-start | bytes 49156
  0.7 9.5 %copy-start.12 = (bf16[768,8]{0,1:T(8,128)(2,1)S(1)}, bf16[768,8]{0,1:T(8,128)(2,1)}, u32[]{:S(2)}) copy-start(bf16[768,8]{0,1:T(8,128)(2,1)} %param.31) | copy-start | bytes 36868
  0.7 10.4 %copy-start.9 = (s32[144]{0:T(256)S(1)}, s32[144]{0:T(256)}, u32[]{:S(2)}) copy-start(s32[144]{0:T(256)} %param.24) | copy-start | bytes 1732
  0.7 10.4 %copy-start.10 = (s32[2,8]{1,0:T(2,128)S(1)}, s32[2,8]{1,0:T(2,128)}, u32[]{:S(2)}) copy-start(s32[2,8]{1,0:T(2,128)} %param.23) | copy-start | bytes 196
  49.9 1.7 %copy-start.2 = (f32[2,8,144,128]{3,2,1,0:T(8,128)S(1)}, f32[2,8,144,128]{3,2,1,0:T(8,128)}, u32[]{:S(2)}) copy-start(f32[2,8,144,128]{3,2,1,0:T(8,128)} %param.20) | copy-start | bytes 3538948
  51.6 2.0 %copy-start.8 = (f32[128,12]{0,1:T(8,128)S(1)}, f32[128,12]{0,1:T(8,128)}, u32[]{:S(2)}) copy-start(f32[128,12]{0,1:T(8,128)} %param.33) | copy-start | bytes 18436
  53.6 2.6 %copy-start.1 = (f32[2,8,144,128]{3,2,1,0:T(8,128)}, f32[2,8,144,128]{3,2,1,0:T(8,128)S(1)}, u32[]{:S(2)}) copy-start(f32[2,8,144,128]{3,2,1,0:T(8,128)S(1)} %fusion.3) | copy-start | bytes 3538948
  53.6 2.0 %copy-start.6 = (bf16[2,8,12,64]{3,1,0,2:T(8,128)(2,1)S(1)}, bf16[2,8,12,64]{3,1,0,2:T(8,128)(2,1)}, u32[]{:S(2)}) copy-start(bf16[2,8,12,64]{3,1,0,2:T(8,128)(2,1)} %copy.36) | copy-start | bytes 73732
  53.7 2.0 %copy-start.11 = (f32[12]{0:T(128)S(1)}, f32[12]{0:T(128)}, u32[]{:S(2)}) copy-start(f32[12]{0:T(128)} %param.34) | copy-start | bytes 148
  53.7 2.2 %copy-start.5 = (bf16[144,768]{0,1:T(8,128)(2,1)S(1)}, bf16[144,768]{0,1:T(8,128)(2,1)}, u32[]{:S(2)}) copy-start(bf16[144,768]{0,1:T(8,128)(2,1)} %copy.40) | copy-start | bytes 663556
  148.8 3.4 %copy-start.3 = (bf16[768,768]{1,0:T(8,128)(2,1)S(1)}, bf16[768,768]{1,0:T(8,128)(2,1)}, u32[]{:S(2)}) copy-start(bf16[768,768]{1,0:T(8,128)(2,1)} %param.37) | copy-start | bytes 3538948
where the time goes:
time: 154 us; the launch traced here: 153 us
  blocking collectives  128 us (83%)
  matrix products  9.65 us (6%)
  other arithmetic  7.11 us (5%)
  local copies, waits for them, and re-layouts  5.97 us (4%)
  between operations  1.64 us (1%)
    all_gather x3, blocking collectives, combined_all(): gathered = jax.tree.map(lambda a: lax.all_gather(a, axis), part)  92.1 us
    all_gather x1, blocking collectives, on_device(): query_gate = lax.all_gather(query_part, 'col', axis=2, tiled=True)  34 us
    dot_general x3, matrix products, flat_dot(): product = jnp.dot(flat_left, right, preferred_element_type=jnp.float32)  3.08 us

commit v1 on v0

--- a/solution.py
+++ b/solution.py
@@ -1,8 +1,11 @@
+import functools
 import math
 
 import jax
 import jax.numpy as jnp
 from jax import lax
+from jax.experimental import pallas as pl
+from jax.experimental.pallas import tpu as pltpu
 from jax.sharding import PartitionSpec as P
 
 EPSILON = 1e-05
@@ -142,9 +145,366 @@
     return (new_pair, single_update)
 
 
+def iota(shape, axis):
+    return lax.broadcasted_iota(jnp.int32, shape, axis)
+
+
+def dot_nt(left, right, precision=None):
+    return lax.dot_general(
+        left, right, (((1,), (1,)), ((), ())), precision=precision,
+        preferred_element_type=jnp.float32,
+    )
+
+
+def dot_nn(left, right, precision=None):
+    return jnp.dot(left, right, precision=precision, preferred_element_type=jnp.float32)
+
+
+def rounded(value):
+    return value.astype(jnp.bfloat16).astype(jnp.float32)
+
+
+def column_of(row, count):
+    spot = iota((count, row.shape[1]), 0) == iota((count, row.shape[1]), 1)
+    return jnp.sum(jnp.where(spot, row, jnp.zeros_like(row)), axis=1, keepdims=True)
+
+
+def fused_kernel(
+    query_chain, timestep, query_single, key_single, key_chain, query_mask, key_mask,
+    time_table, norm_gain, left_proj, right_proj, outer_proj, bias_proj, chain_weight,
+    pair_hbm, query_proj_hbm, kv_proj_hbm, out_proj_hbm,
+    new_pair_hbm, single_update,
+    pair, fresh, query_proj, kv_proj, out_proj, parts_q, keys_values, bias, mixers,
+    packed, partial, gates, final,
+    load_sem, store_sem, q_send, q_recv, kv_send, kv_recv, p_send, p_recv, f_send, f_recv,
+):
+    cols = lax.axis_size("col")
+    me = lax.axis_index("col")
+    side = lax.axis_index("row")
+    peers = [lax.rem(me + offset, cols) for offset in range(1, cols)]
+
+    barrier = pltpu.get_barrier_semaphore()
+    for peer in peers:
+        pl.semaphore_signal(
+            barrier, inc=1, device_id={"col": peer}, device_id_type=pl.DeviceIdType.MESH
+        )
+    pl.semaphore_signal(
+        barrier, inc=1, device_id={"row": 1 - side}, device_id_type=pl.DeviceIdType.MESH
+    )
+
+    loads = [
+        pltpu.make_async_copy(source, target, load_sem.at[place])
+        for place, (source, target) in enumerate(
+            [
+                (query_proj_hbm, query_proj),
+                (kv_proj_hbm, kv_proj),
+                (pair_hbm, pair),
+                (out_proj_hbm, out_proj),
+            ]
+        )
+    ]
+    for load in loads:
+        load.start()
+
+    slabs, slab_rows, width = query_single.shape
+    rows = slabs * slab_rows
+    keys = key_single.shape[0]
+    steps = time_table.shape[0]
+    rank = left_proj.shape[1]
+    channels = outer_proj.shape[1]
+    heads = chain_weight.shape[1]
+    head_width = width // heads
+    slots = bias.shape[2]
+    own_rows = rows // cols
+
+    def normal(features):
+        average = jnp.mean(features, axis=-1, keepdims=True)
+        centred = features - average
+        spread = jnp.mean(centred * centred, axis=-1, keepdims=True)
+        return (centred * lax.rsqrt(spread + EPSILON) * norm_gain[...]).astype(jnp.bfloat16)
+
+    picked = iota((steps, width), 0) == timestep[0]
+    time_row = jnp.sum(
+        jnp.where(picked, time_table[...].astype(jnp.float32), 0.0), axis=0, keepdims=True
+    )
+
+    query_flags = jnp.concatenate(
+        [
+            column_of(query_mask[slab : slab + 1, :].astype(jnp.float32), slab_rows)
+            for slab in range(slabs)
+        ],
+        axis=0,
+    )
+    query_norm = normal(
+        query_single[...].astype(jnp.float32).reshape(rows, width) + query_flags * time_row
+    )
+    loads[0].wait()
+    parts_q[me] = dot_nn(query_norm, query_proj[...]).astype(jnp.bfloat16)
+
+    pl.semaphore_wait(barrier, cols)
+    q_copies = [
+        pltpu.make_async_remote_copy(
+            src_ref=parts_q.at[me], dst_ref=parts_q.at[me],
+            send_sem=q_send.at[place], recv_sem=q_recv.at[place],
+            device_id={"col": peer}, device_id_type=pl.DeviceIdType.MESH,
+        )
+        for place, peer in enumerate(peers)
+    ]
+    for copy in q_copies:
+        copy.start()
+
+    key_flags = column_of(key_mask[...].astype(jnp.float32), keys)
+    key_norm = normal(key_single[...].astype(jnp.float32) + key_flags * time_row)
+    loads[1].wait()
+    keys_values[side] = dot_nn(key_norm, kv_proj[...]).astype(jnp.bfloat16)
+    kv_copy = pltpu.make_async_remote_copy(
+        src_ref=keys_values.at[side], dst_ref=keys_values.at[side],
+        send_sem=kv_send, recv_sem=kv_recv,
+        device_id={"row": 1 - side}, device_id_type=pl.DeviceIdType.MESH,
+    )
+    kv_copy.start()
+
+    left_factor = dot_nn(query_norm, left_proj[...])
+    right_factor = dot_nn(key_norm, right_proj[...])
+    square = rank * rank
+    spread_left = (iota((rank, square), 1) // rank == iota((rank, square), 0)).astype(jnp.float32)
+    left_wide = dot_nn(left_factor, spread_left, HIGHEST)
+    on_rank = iota((rows, rank, square), 2) % rank == iota((rows, rank, square), 1)
+    left_blocks = jnp.where(on_rank, left_wide[:, None, :], 0.0).reshape(rows * rank, square)
+    mixer = dot_nn(left_blocks, outer_proj[...].astype(jnp.float32), HIGHEST)
+    mixer = mixer.reshape(rows, rank, channels)
+
+    terms = 6
+    tile_right = (iota((rank, terms * rank), 1) % rank == iota((rank, terms * rank), 0)).astype(
+        jnp.float32
+    )
+    right_wide = dot_nn(right_factor, tile_right, HIGHEST)
+    right_1 = rounded(right_wide)
+    right_2 = rounded(right_wide - right_1)
+    right_3 = right_wide - right_1 - right_2
+    group = iota(right_wide.shape, 1) // rank
+    right_terms = jnp.where(
+        group < 3, right_1, jnp.where(group < 5, right_2, right_3)
+    ).astype(jnp.bfloat16)
+    mixer_1 = rounded(mixer)
+    mixer_2 = rounded(mixer - mixer_1)
+    mixer_3 = mixer - mixer_1 - mixer_2
+    mixers[...] = jnp.concatenate(
+        [mixer_1, mixer_2, mixer_3, mixer_1, mixer_2, mixer_1], axis=1
+    ).astype(jnp.bfloat16)
+
+    head_spot = (iota((slots, heads), 0) == iota((slots, heads), 1)).astype(jnp.float32)
+    bias_rows = dot_nt(head_spot, bias_proj[...], HIGHEST)
+    bias_1 = rounded(bias_rows)
+    bias_2 = bias_rows - bias_1
+    bias_terms = jnp.concatenate(
+        [
+            jnp.concatenate([bias_1, bias_1], axis=1),
+            jnp.concatenate([bias_2, bias_2], axis=1),
+        ],
+        axis=0,
+    ).astype(jnp.bfloat16)
+    chain_column = column_of(chain_weight[...], slots)
+    chains = key_chain[...]
+
+    loads[2].wait()
+
+    def update_row(row, carry):
+        slab = row // slab_rows
+        place = row - slab * slab_rows
+        updated = pair[slab, place] + dot_nn(right_terms, mixers[row])
+        fresh[slab, place] = updated
+        upper = rounded(updated)
+        both = jnp.concatenate([upper, updated - upper], axis=1).astype(jnp.bfloat16)
+        logits = dot_nt(bias_terms, both)
+        differ = (chains != query_chain[slab, place]).astype(jnp.float32)
+        bias[slab, place] = logits[:slots] + logits[slots:] + chain_column * differ
+        return carry
+
+    lax.fori_loop(0, rows, update_row, 0, unroll=UNROLL)
+    store = pltpu.make_async_copy(fresh, new_pair_hbm, store_sem)
+    store.start()
+
+    for copy in q_copies:
+        copy.wait()
+    half = cols // 2
+    query = jnp.concatenate(
+        [parts_q[place].astype(jnp.float32) for place in range(half)], axis=1
+    )
+    gate = jax.nn.sigmoid(
+        jnp.concatenate(
+            [parts_q[place].astype(jnp.float32) for place in range(half, cols)], axis=1
+        )
+    )
+    for place in range(cols):
+        gates[place] = gate[place * own_rows : (place + 1) * own_rows]
+    on_head = iota((rows, slots, width), 2) // head_width == iota((rows, slots, width), 1)
+    query_blocks = (
+        jnp.where(on_head, query[:, None, :], 0.0)
+        .reshape(rows * slots, width)
+        .astype(jnp.bfloat16)
+    )
+    kv_copy.wait()
+    scores = dot_nt(query_blocks, keys_values[0]) * (1.0 / math.sqrt(head_width)) + bias[
+        ...
+    ].reshape(rows * slots, keys)
+    maxima = jnp.max(scores, axis=1, keepdims=True)
+    exponent = jnp.exp(scores - maxima)
+    totals = jnp.sum(exponent, axis=1, keepdims=True)
+    summed = dot_nn(exponent.astype(jnp.bfloat16), keys_values[1]).reshape(rows, slots, width)
+    summed = jnp.sum(jnp.where(on_head, summed, 0.0), axis=1)
+    on_lane = iota((rows, slots, LANES), 2) == iota((rows, slots, LANES), 1)
+
+    def by_lane(column):
+        return jnp.sum(jnp.where(on_lane, column.reshape(rows, slots, 1), 0.0), axis=1)
+
+    bundle = jnp.concatenate([summed, by_lane(maxima), by_lane(totals)], axis=1)
+    for place in range(cols):
+        packed[place] = bundle[place * own_rows : (place + 1) * own_rows]
+    p_copies = [
+        pltpu.make_async_remote_copy(
+            src_ref=packed.at[peer], dst_ref=partial.at[me],
+            send_sem=p_send.at[place], recv_sem=p_recv.at[place],
+            device_id={"col": peer}, device_id_type=pl.DeviceIdType.MESH,
+        )
+        for place, peer in enumerate(peers)
+    ]
+    for copy in p_copies:
+        copy.start()
+    partial[me] = packed[me]
+    gate_own = gates[me]
+    spread_heads = (
+        (iota((LANES, width), 1) // head_width == iota((LANES, width), 0))
+        .astype(jnp.float32)
+    )
+    loads[3].wait()
+    for copy in p_copies:
+        copy.wait()
+
+    maxima = [partial[place, :, width : width + LANES] for place in range(cols)]
+    totals = [partial[place, :, width + LANES :] for place in range(cols)]
+    peak = functools.reduce(jnp.maximum, maxima)
+    scales = [jnp.exp(part - peak) for part in maxima]
+    total = functools.reduce(jnp.add, [a * b for a, b in zip(totals, scales)])
+    total = jnp.where(iota(total.shape, 1) < heads, total, 1.0)
+    shares = dot_nn(
+        jnp.concatenate([scale / total for scale in scales], axis=0), spread_heads, HIGHEST
+    )
+    joint = functools.reduce(
+        jnp.add,
+        [
+            shares[place * own_rows : (place + 1) * own_rows] * partial[place, :, :width]
+            for place in range(cols)
+        ],
+    )
+    attended = joint * gate_own
+    attended = jnp.concatenate(
+        [attended, jnp.zeros((rows - own_rows, width), jnp.float32)], axis=0
+    ).astype(jnp.bfloat16)
+
+    final[me] = rounded(dot_nn(attended, out_proj[...])[:own_rows])
+    f_copies = [
+        pltpu.make_async_remote_copy(
+            src_ref=final.at[me], dst_ref=final.at[me],
+            send_sem=f_send.at[place], recv_sem=f_recv.at[place],
+            device_id={"col": peer}, device_id_type=pl.DeviceIdType.MESH,
+        )
+        for place, peer in enumerate(peers)
+    ]
+    for copy in f_copies:
+        copy.start()
+    store.wait()
+    for copy in f_copies:
+        copy.wait()
+    single_update[...] = (
+        jnp.concatenate([final[place] for place in range(cols)], axis=0)
+        .reshape(slabs, slab_rows, width)
+        .astype(jnp.bfloat16)
+    )
+
+
+LANES = 128
+UNROLL = 4
+
+
+def fused(
+    pair_block, query_single, key_single, query_chain, key_chain, query_mask, key_mask,
+    timestep, time_table, norm_gain, left_proj, right_proj, outer_proj, bias_proj,
+    chain_weight, query_proj, kv_proj, out_proj,
+):
+    cols = lax.axis_size("col")
+    slabs, slab_rows, width = query_single.shape
+    rows = slabs * slab_rows
+    keys = key_single.shape[0]
+    heads = chain_weight.shape[0]
+    slots = -(-heads // 16) * 16
+    rank = left_proj.shape[1]
+    own_rows = rows // cols
+    vmem = pl.BlockSpec(memory_space=pltpu.VMEM)
+    smem = pl.BlockSpec(memory_space=pltpu.SMEM)
+    anywhere = pl.BlockSpec(memory_space=pl.ANY)
+    dma = pltpu.SemaphoreType.DMA
+    return pl.pallas_call(
+        fused_kernel,
+        out_shape=(
+            jax.ShapeDtypeStruct(pair_block.shape, jnp.float32),
+            jax.ShapeDtypeStruct(query_single.shape, jnp.bfloat16),
+        ),
+        in_specs=[smem, smem] + [vmem] * 12 + [anywhere] * 4,
+        out_specs=(anywhere, vmem),
+        scratch_shapes=[
+            pltpu.VMEM(pair_block.shape, jnp.float32),
+            pltpu.VMEM(pair_block.shape, jnp.float32),
+            pltpu.VMEM(query_proj.shape, jnp.bfloat16),
+            pltpu.VMEM(kv_proj.shape, jnp.bfloat16),
+            pltpu.VMEM(out_proj.shape, jnp.bfloat16),
+            pltpu.VMEM((cols, rows, query_proj.shape[1]), jnp.bfloat16),
+            pltpu.VMEM((2, keys, width), jnp.bfloat16),
+            pltpu.VMEM((slabs, slab_rows, slots, keys), jnp.float32),
+            pltpu.VMEM((rows, 6 * rank, outer_proj.shape[1]), jnp.bfloat16),
+            pltpu.VMEM((cols, own_rows, width + 2 * LANES), jnp.float32),
+            pltpu.VMEM((cols, own_rows, width + 2 * LANES), jnp.float32),
+            pltpu.VMEM((cols, own_rows, width), jnp.float32),
+            pltpu.VMEM((cols, own_rows, width), jnp.float32),
+            dma((4,)),
+            dma,
+            dma((cols - 1,)),
+            dma((cols - 1,)),
+            dma,
+            dma,
+            dma((cols - 1,)),
+            dma((cols - 1,)),
+            dma((cols - 1,)),
+            dma((cols - 1,)),
+        ],
+        compiler_params=pltpu.CompilerParams(
+            collective_id=0, has_side_effects=True, vmem_limit_bytes=48 * 1024 * 1024
+        ),
+    )(
+        query_chain, timestep, query_single, key_single, key_chain.reshape(1, -1), query_mask,
+        key_mask.reshape(1, -1), time_table, norm_gain.reshape(1, -1), left_proj, right_proj,
+        outer_proj, bias_proj, chain_weight.reshape(1, -1), pair_block, query_proj, kv_proj,
+        out_proj,
+    )
+
+
+def serve(*arrays):
+    query_single, chain_weight, kv_proj = arrays[1], arrays[14], arrays[16]
+    rows = query_single.shape[0] * query_single.shape[1]
+    cols = lax.axis_size("col")
+    fits = (
+        rows % cols == 0
+        and cols % 2 == 0
+        and lax.axis_size("row") == 2
+        and kv_proj.shape[1] == query_single.shape[2]
+        and chain_weight.shape[0] <= LANES
+    )
+    return fused(*arrays) if fits else on_device(*arrays)
+
+
 def solution(mesh):
     return jax.shard_map(
-        on_device,
+        serve,
         mesh=mesh,
         in_specs=(
             P("grp", "row", "col", None),

time: 154 us -> 34.1 us (0.22)
  blocking collectives: 128 us -> 0 us
  Pallas kernels: 0 us -> 20.1 us
  matrix products: 9.65 us -> 0 us
  other arithmetic: 7.11 us -> 0 us
  local copies, waits for them, and re-layouts: 5.97 us -> 11.9 us
    all_gather x5 -> x0, blocking collectives: 128 us -> none  [the longest x3 92.1 us: combined_all(): gathered = jax.tree.map(lambda a: lax.all_gather(a, axis), part)]
    pallas_call x0 -> x1, Pallas kernels: none -> 20.1 us  [fused(): pl.pallas_call(fused_kernel, out_shape=(jax.ShapeDtypeStruct(pair_block.s...]
    unnamed x29 -> x30, local copies, waits for them, and re-layouts: 0.35 us -> 11.2 us
    dot_general x8 -> x0, matrix products: 9.11 us -> none  [the longest x3 3.08 us: flat_dot(): product = jnp.dot(flat_left, right, preferred_element_type=jnp.float32)]
    reduce_sum x6 -> x0, other arithmetic: 5.35 us -> none  [the longest x2 2.1 us: normalize(): spread = jnp.mean(centred * centred, axis=-1, keepdims=True)]
    slice x4 -> x0, local copies, waits for them, and re-layouts: 1.65 us -> none  [the longest x2 0.94 us: on_device(): keys_values[:, model_width:].reshape(key_count, heads, head_size)]
where the time goes in v1:
time: 34.1 us; the launch traced here: 33.5 us
  Pallas kernels  20.1 us (59%)
  local copies, waits for them, and re-layouts  11.9 us (35%)
  between operations  1.51 us (4%)
    pallas_call x1, Pallas kernels, fused(): pl.pallas_call(fused_kernel, out_shape=(jax.ShapeDtypeStruct(pair_block.s...  20.1 us
    unnamed x30, local copies, waits for them, and re-layouts  11.2 us
    reshape x1, local copies, waits for them, and re-layouts, fused(): norm_gain.reshape(1, -1)  0.69 us

profile of v1, /device:TPU:0, one launch (start us, length us, event | category | flops | bytes accessed | tf_op | source)
XLA Modules:
  0.0 33.5 jit_solution(10881930713295895269)
XLA Ops:
  0.6 0.0 copy-start.11
  0.6 0.0 copy-start.10
  0.7 0.0 copy-start.9
  0.7 0.0 copy-start.8
  0.7 0.0 copy-start.7
  0.7 0.0 copy-start
  1.4 0.7 %reshape.18.norm_gain = f32[1,768]{1,0:T(1,128)S(1)} reshape(f32[768]{0:T(1024)} %param.27) | data formatting | bytes 6144 | tf_op jit(solution)/shard_map/reshape | solution.py:485
  2.1 0.8 %copy.22.bias_proj = f32[128,12]{1,0:T(8,128)S(1)} copy(f32[128,12]{0,1:T(8,128)} %param.31) | data formatting | bytes 12288 | tf_op args[13]
  2.9 0.9 %copy.20.left_proj = bf16[768,8]{1,0:T(8,128)(2,1)S(1)} copy(bf16[768,8]{0,1:T(8,128)(2,1)} %param.28) | data formatting | bytes 24576 | tf_op args[10]
  3.8 0.9 %copy.21.right_proj = bf16[768,8]{1,0:T(8,128)(2,1)S(1)} copy(bf16[768,8]{0,1:T(8,128)(2,1)} %param.29) | data formatting | bytes 24576 | tf_op args[11]
  4.7 1.1 %copy.23.query_proj_hbm = bf16[768,192]{1,0:T(8,128)(2,1)S(1)} copy(bf16[768,192]{0,1:T(8,128)(2,1)} %param.33) | data formatting | bytes 589824 | tf_op args[15]
  5.9 0.0 copy-done.11
  5.9 0.0 copy-done.10
  5.9 0.0 copy-done.9
  5.9 0.0 copy-done.8
  5.9 0.0 copy-done.7
  5.9 0.0 copy-done
  5.9 0.0 copy-start.1
  5.9 1.3 %copy-done.1 = bf16[768,768]{1,0:T(8,128)(2,1)S(1)} copy-done((bf16[768,768]{1,0:T(8,128)(2,1)S(1)}, bf16[768,768]{1,0:T(8,128)(2,1)}, u32[]{:S(2)}) %copy-start.1) | copy-done | bytes 1179672
  7.2 0.0 copy-start.2
  7.2 1.3 %copy-done.2 = bf16[768,768]{1,0:T(8,128)(2,1)S(1)} copy-done((bf16[768,768]{1,0:T(8,128)(2,1)S(1)}, bf16[768,768]{1,0:T(8,128)(2,1)}, u32[]{:S(2)}) %copy-start.2) | copy-done | bytes 1179672
  8.5 0.0 copy-start.3
  8.5 0.9 %copy-done.3 = bf16[144,768]{1,0:T(8,128)(2,1)S(1)} copy-done((bf16[144,768]{1,0:T(8,128)(2,1)S(1)}, bf16[144,768]{1,0:T(8,128)(2,1)}, u32[]{:S(2)}) %copy-start.3) | copy-done | bytes 221208
  9.4 0.0 copy-start.4
  9.4 0.9 %copy-done.4 = bf16[50,768]{1,0:T(8,128)(2,1)S(1)} copy-done((bf16[50,768]{1,0:T(8,128)(2,1)S(1)}, bf16[50,768]{1,0:T(8,128)(2,1)}, u32[]{:S(2)}) %copy-start.4) | copy-done | bytes 76824
  10.3 0.0 copy-start.5
  10.3 0.7 %copy-done.5 = bf16[2,8,768]{2,1,0:T(8,128)(2,1)S(1)} copy-done((bf16[2,8,768]{2,1,0:T(8,128)(2,1)S(1)}, bf16[2,8,768]{2,1,0:T(8,128)(2,1)}, u32[]{:S(2)}) %copy-start.5) | copy-done | bytes 24600
  11.0 0.0 copy-start.6
  11.0 0.7 %copy-done.6 = bf16[64,128]{1,0:T(8,128)(2,1)S(1)} copy-done((bf16[64,128]{1,0:T(8,128)(2,1)S(1)}, bf16[64,128]{1,0:T(8,128)(2,1)}, u32[]{:S(2)}) %copy-start.6) | copy-done | bytes 16408
  11.7 20.1 %shard_map.185 = (f32[2,8,144,128]{3,2,1,0:T(8,128)S(1)}, bf16[2,8,768]{2,1,0:T(8,128)(2,1)S(1)}) custom-call(s32[2,8]{1,0:T(2,128)S(1)} %copy-done.7, s32[1]{0:T(128)S(6)} %copy.26.timestep, bf16[2,8,768]{2,1,0:T(8,128)(2,1)S(1)} %copy-done.5, bf16[144,768]{1,0:T(8,128)(2,1)S(1)} %copy-done.3, s32[1,144]{1,0:T(1,128)S(1)} %bitcast.3, s32[2,8]{1,0:T(2,128)S(1)} %copy-done.9, ...), custom_call_target="tpu_custom_call" | custom-call | tf_op jit(solution)/shard_map/pallas_call | solution.py:447
  31.9 1.0 %copy.27 = f32[2,8,144,128]{3,2,1,0:T(8,128)} copy(f32[2,8,144,128]{3,2,1,0:T(8,128)S(1)} %get-tuple-element.4) | data formatting | bytes 2359296
  32.9 0.6 %copy.28 = bf16[2,8,768]{2,1,0:T(8,128)(2,1)} copy(bf16[2,8,768]{2,1,0:T(8,128)(2,1)S(1)} %get-tuple-element.5) | data formatting | bytes 49152
Async XLA Ops:
  0.6 5.2 %copy-start.11 = (f32[12]{0:T(128)S(1)}, f32[12]{0:T(128)}, u32[]{:S(2)}) copy-start(f32[12]{0:T(128)} %param.32) | copy-start | bytes 148
  0.6 5.2 %copy-start.10 = (s32[144]{0:T(256)S(1)}, s32[144]{0:T(256)}, u32[]{:S(2)}) copy-start(s32[144]{0:T(256)} %param.24) | copy-start | bytes 1732
  0.7 5.2 %copy-start.9 = (s32[2,8]{1,0:T(2,128)S(1)}, s32[2,8]{1,0:T(2,128)}, u32[]{:S(2)}) copy-start(s32[2,8]{1,0:T(2,128)} %query_mask.1) | copy-start | bytes 196
  0.7 5.2 %copy-start.8 = (s32[144]{0:T(256)S(1)}, s32[144]{0:T(256)}, u32[]{:S(2)}) copy-start(s32[144]{0:T(256)} %param.22) | copy-start | bytes 1732
  0.7 5.2 %copy-start.7 = (s32[2,8]{1,0:T(2,128)S(1)}, s32[2,8]{1,0:T(2,128)}, u32[]{:S(2)}) copy-start(s32[2,8]{1,0:T(2,128)} %query_chain.1) | copy-start | bytes 196
  0.7 5.2 %copy-start = (f32[2,8,144,128]{3,2,1,0:T(8,128)S(1)}, f32[2,8,144,128]{3,2,1,0:T(8,128)}, u32[]{:S(2)}) copy-start(f32[2,8,144,128]{3,2,1,0:T(8,128)} %pair_hbm.1) | copy-start | bytes 3538948
  5.9 1.3 %copy-start.1 = (bf16[768,768]{1,0:T(8,128)(2,1)S(1)}, bf16[768,768]{1,0:T(8,128)(2,1)}, u32[]{:S(2)}) copy-start(bf16[768,768]{1,0:T(8,128)(2,1)} %kv_proj_hbm.1) | copy-start | bytes 3538948
  7.2 1.3 %copy-start.2 = (bf16[768,768]{1,0:T(8,128)(2,1)S(1)}, bf16[768,768]{1,0:T(8,128)(2,1)}, u32[]{:S(2)}) copy-start(bf16[768,768]{1,0:T(8,128)(2,1)} %out_proj_hbm.1) | copy-start | bytes 3538948
  8.5 0.9 %copy-start.3 = (bf16[144,768]{1,0:T(8,128)(2,1)S(1)}, bf16[144,768]{1,0:T(8,128)(2,1)}, u32[]{:S(2)}) copy-start(bf16[144,768]{1,0:T(8,128)(2,1)} %key_single.1) | copy-start | bytes 663556
  9.4 0.9 %copy-start.4 = (bf16[50,768]{1,0:T(8,128)(2,1)S(1)}, bf16[50,768]{1,0:T(8,128)(2,1)}, u32[]{:S(2)}) copy-start(bf16[50,768]{1,0:T(8,128)(2,1)} %time_table.1) | copy-start | bytes 230404
  10.3 0.7 %copy-start.5 = (bf16[2,8,768]{2,1,0:T(8,128)(2,1)S(1)}, bf16[2,8,768]{2,1,0:T(8,128)(2,1)}, u32[]{:S(2)}) copy-start(bf16[2,8,768]{2,1,0:T(8,128)(2,1)} %query_single.1) | copy-start | bytes 73732
  11.0 0.7 %copy-start.6 = (bf16[64,128]{1,0:T(8,128)(2,1)S(1)}, bf16[64,128]{1,0:T(8,128)(2,1)}, u32[]{:S(2)}) copy-start(bf16[64,128]{1,0:T(8,128)(2,1)} %outer_proj.1) | copy-start | bytes 49156

commit v2 on v1

--- a/solution.py
+++ b/solution.py
@@ -170,18 +170,31 @@
 
 
 def fused_kernel(
-    query_chain, timestep, query_single, key_single, key_chain, query_mask, key_mask,
-    time_table, norm_gain, left_proj, right_proj, outer_proj, bias_proj, chain_weight,
-    pair_hbm, query_proj_hbm, kv_proj_hbm, out_proj_hbm,
-    new_pair_hbm, single_update,
-    pair, fresh, query_proj, kv_proj, out_proj, parts_q, keys_values, bias, mixers,
-    packed, partial, gates, final,
-    load_sem, store_sem, q_send, q_recv, kv_send, kv_recv, p_send, p_recv, f_send, f_recv,
+    query_chain, timestep, *operands_results_scratch
 ):
+    sources = operands_results_scratch[:OPERANDS]
+    new_pair_hbm, single_update = operands_results_scratch[OPERANDS : OPERANDS + 2]
+    targets = operands_results_scratch[OPERANDS + 2 : 2 * OPERANDS + 2]
+    (
+        time_table, query_single, query_mask, norm_gain, query_proj, key_single, key_mask,
+        kv_proj, left_proj, right_proj, outer_proj, bias_proj, chain_weight, key_chain, pair,
+        out_proj,
+    ) = targets
+    (
+        fresh, parts_q, keys_values, bias, packed, partial, gates, final,
+        load_sem, store_sem, q_send, q_recv, kv_send, kv_recv, p_send, p_recv, f_send, f_recv,
+    ) = operands_results_scratch[2 * OPERANDS + 2 :]
     cols = lax.axis_size("col")
     me = lax.axis_index("col")
     side = lax.axis_index("row")
     peers = [lax.rem(me + offset, cols) for offset in range(1, cols)]
+
+    loads = [
+        pltpu.make_async_copy(source, target, load_sem.at[place])
+        for place, (source, target) in enumerate(zip(sources, targets))
+    ]
+    for load in loads:
+        load.start()
 
     barrier = pltpu.get_barrier_semaphore()
     for peer in peers:
@@ -192,36 +205,28 @@
         barrier, inc=1, device_id={"row": 1 - side}, device_id_type=pl.DeviceIdType.MESH
     )
 
-    loads = [
-        pltpu.make_async_copy(source, target, load_sem.at[place])
-        for place, (source, target) in enumerate(
-            [
-                (query_proj_hbm, query_proj),
-                (kv_proj_hbm, kv_proj),
-                (pair_hbm, pair),
-                (out_proj_hbm, out_proj),
-            ]
-        )
-    ]
-    for load in loads:
-        load.start()
-
     slabs, slab_rows, width = query_single.shape
     rows = slabs * slab_rows
     keys = key_single.shape[0]
     steps = time_table.shape[0]
-    rank = left_proj.shape[1]
+    rank = left_proj.shape[0]
     channels = outer_proj.shape[1]
     heads = chain_weight.shape[1]
     head_width = width // heads
     slots = bias.shape[2]
     own_rows = rows // cols
 
+    for load in loads[:4]:
+        load.wait()
+    gain = jnp.concatenate(
+        [norm_gain[place : place + 1] for place in range(norm_gain.shape[0])], axis=1
+    )
+
     def normal(features):
         average = jnp.mean(features, axis=-1, keepdims=True)
         centred = features - average
         spread = jnp.mean(centred * centred, axis=-1, keepdims=True)
-        return (centred * lax.rsqrt(spread + EPSILON) * norm_gain[...]).astype(jnp.bfloat16)
+        return (centred * lax.rsqrt(spread + EPSILON) * gain).astype(jnp.bfloat16)
 
     picked = iota((steps, width), 0) == timestep[0]
     time_row = jnp.sum(
@@ -238,8 +243,8 @@
     query_norm = normal(
         query_single[...].astype(jnp.float32).reshape(rows, width) + query_flags * time_row
     )
-    loads[0].wait()
-    parts_q[me] = dot_nn(query_norm, query_proj[...]).astype(jnp.bfloat16)
+    loads[4].wait()
+    parts_q[me] = dot_nt(query_norm, query_proj[...]).astype(jnp.bfloat16)
 
     pl.semaphore_wait(barrier, cols)
     q_copies = [
@@ -253,9 +258,11 @@
     for copy in q_copies:
         copy.start()
 
+    loads[5].wait()
+    loads[6].wait()
     key_flags = column_of(key_mask[...].astype(jnp.float32), keys)
     key_norm = normal(key_single[...].astype(jnp.float32) + key_flags * time_row)
-    loads[1].wait()
+    loads[7].wait()
     keys_values[side] = dot_nn(key_norm, kv_proj[...]).astype(jnp.bfloat16)
     kv_copy = pltpu.make_async_remote_copy(
         src_ref=keys_values.at[side], dst_ref=keys_values.at[side],
@@ -264,15 +271,19 @@
     )
     kv_copy.start()
 
-    left_factor = dot_nn(query_norm, left_proj[...])
-    right_factor = dot_nn(key_norm, right_proj[...])
+    for load in loads[8:14]:
+        load.wait()
+    left_factor = dot_nt(query_norm, left_proj[...])
+    right_factor = dot_nt(key_norm, right_proj[...])
     square = rank * rank
     spread_left = (iota((rank, square), 1) // rank == iota((rank, square), 0)).astype(jnp.float32)
     left_wide = dot_nn(left_factor, spread_left, HIGHEST)
     on_rank = iota((rows, rank, square), 2) % rank == iota((rows, rank, square), 1)
     left_blocks = jnp.where(on_rank, left_wide[:, None, :], 0.0).reshape(rows * rank, square)
     mixer = dot_nn(left_blocks, outer_proj[...].astype(jnp.float32), HIGHEST)
-    mixer = mixer.reshape(rows, rank, channels)
+    mixer = jnp.concatenate(
+        [mixer[row * rank : (row + 1) * rank] for row in range(rows)], axis=1
+    )
 
     terms = 6
     tile_right = (iota((rank, terms * rank), 1) % rank == iota((rank, terms * rank), 0)).astype(
@@ -289,12 +300,12 @@
     mixer_1 = rounded(mixer)
     mixer_2 = rounded(mixer - mixer_1)
     mixer_3 = mixer - mixer_1 - mixer_2
-    mixers[...] = jnp.concatenate(
-        [mixer_1, mixer_2, mixer_3, mixer_1, mixer_2, mixer_1], axis=1
+    mixer_terms = jnp.concatenate(
+        [mixer_1, mixer_2, mixer_3, mixer_1, mixer_2, mixer_1], axis=0
     ).astype(jnp.bfloat16)
 
     head_spot = (iota((slots, heads), 0) == iota((slots, heads), 1)).astype(jnp.float32)
-    bias_rows = dot_nt(head_spot, bias_proj[...], HIGHEST)
+    bias_rows = dot_nn(head_spot, bias_proj[...], HIGHEST)
     bias_1 = rounded(bias_rows)
     bias_2 = bias_rows - bias_1
     bias_terms = jnp.concatenate(
@@ -307,21 +318,18 @@
     chain_column = column_of(chain_weight[...], slots)
     chains = key_chain[...]
 
-    loads[2].wait()
-
-    def update_row(row, carry):
-        slab = row // slab_rows
-        place = row - slab * slab_rows
-        updated = pair[slab, place] + dot_nn(right_terms, mixers[row])
+    loads[14].wait()
+    change = dot_nn(right_terms, mixer_terms)
+    for row in range(rows):
+        slab, place = row // slab_rows, row % slab_rows
+        updated = pair[slab, place] + change[:, row * channels : (row + 1) * channels]
         fresh[slab, place] = updated
         upper = rounded(updated)
         both = jnp.concatenate([upper, updated - upper], axis=1).astype(jnp.bfloat16)
         logits = dot_nt(bias_terms, both)
         differ = (chains != query_chain[slab, place]).astype(jnp.float32)
         bias[slab, place] = logits[:slots] + logits[slots:] + chain_column * differ
-        return carry
-
-    lax.fori_loop(0, rows, update_row, 0, unroll=UNROLL)
+
     store = pltpu.make_async_copy(fresh, new_pair_hbm, store_sem)
     store.start()
 
@@ -377,7 +385,7 @@
         (iota((LANES, width), 1) // head_width == iota((LANES, width), 0))
         .astype(jnp.float32)
     )
-    loads[3].wait()
+    loads[15].wait()
     for copy in p_copies:
         copy.wait()
 
@@ -424,7 +432,7 @@
 
 
 LANES = 128
-UNROLL = 4
+OPERANDS = 16
 
 
 def fused(
@@ -438,11 +446,14 @@
     keys = key_single.shape[0]
     heads = chain_weight.shape[0]
     slots = -(-heads // 16) * 16
-    rank = left_proj.shape[1]
     own_rows = rows // cols
-    vmem = pl.BlockSpec(memory_space=pltpu.VMEM)
+    operands = (
+        time_table, query_single, query_mask, norm_gain.reshape(-1, LANES), query_proj.T,
+        key_single, key_mask.reshape(1, -1), kv_proj, left_proj.T, right_proj.T, outer_proj,
+        bias_proj.T, chain_weight.reshape(1, -1), key_chain.reshape(1, -1), pair_block, out_proj,
+    )
     smem = pl.BlockSpec(memory_space=pltpu.SMEM)
-    anywhere = pl.BlockSpec(memory_space=pl.ANY)
+    far = pl.BlockSpec(memory_space=pltpu.HBM)
     dma = pltpu.SemaphoreType.DMA
     return pl.pallas_call(
         fused_kernel,
@@ -450,23 +461,19 @@
             jax.ShapeDtypeStruct(pair_block.shape, jnp.float32),
             jax.ShapeDtypeStruct(query_single.shape, jnp.bfloat16),
         ),
-        in_specs=[smem, smem] + [vmem] * 12 + [anywhere] * 4,
-        out_specs=(anywhere, vmem),
-        scratch_shapes=[
+        in_specs=[smem, smem] + [far] * len(operands),
+        out_specs=(far, pl.BlockSpec(memory_space=pltpu.VMEM)),
+        scratch_shapes=[pltpu.VMEM(operand.shape, operand.dtype) for operand in operands]
+        + [
             pltpu.VMEM(pair_block.shape, jnp.float32),
-            pltpu.VMEM(pair_block.shape, jnp.float32),
-            pltpu.VMEM(query_proj.shape, jnp.bfloat16),
-            pltpu.VMEM(kv_proj.shape, jnp.bfloat16),
-            pltpu.VMEM(out_proj.shape, jnp.bfloat16),
             pltpu.VMEM((cols, rows, query_proj.shape[1]), jnp.bfloat16),
             pltpu.VMEM((2, keys, width), jnp.bfloat16),
             pltpu.VMEM((slabs, slab_rows, slots, keys), jnp.float32),
-            pltpu.VMEM((rows, 6 * rank, outer_proj.shape[1]), jnp.bfloat16),
             pltpu.VMEM((cols, own_rows, width + 2 * LANES), jnp.float32),
             pltpu.VMEM((cols, own_rows, width + 2 * LANES), jnp.float32),
             pltpu.VMEM((cols, own_rows, width), jnp.float32),
             pltpu.VMEM((cols, own_rows, width), jnp.float32),
-            dma((4,)),
+            dma((len(operands),)),
             dma,
             dma((cols - 1,)),
             dma((cols - 1,)),
@@ -478,14 +485,9 @@
             dma((cols - 1,)),
         ],
         compiler_params=pltpu.CompilerParams(
-            collective_id=0, has_side_effects=True, vmem_limit_bytes=48 * 1024 * 1024
+            collective_id=0, has_side_effects=True, vmem_limit_bytes=60 * 1024 * 1024
         ),
-    )(
-        query_chain, timestep, query_single, key_single, key_chain.reshape(1, -1), query_mask,
-        key_mask.reshape(1, -1), time_table, norm_gain.reshape(1, -1), left_proj, right_proj,
-        outer_proj, bias_proj, chain_weight.reshape(1, -1), pair_block, query_proj, kv_proj,
-        out_proj,
-    )
+    )(query_chain, timestep, *operands)
 
 
 def serve(*arrays):
@@ -498,6 +500,7 @@
         and lax.axis_size("row") == 2
         and kv_proj.shape[1] == query_single.shape[2]
         and chain_weight.shape[0] <= LANES
+        and query_single.shape[2] % LANES == 0
     )
     return fused(*arrays) if fits else on_device(*arrays)
 

time: 34.1 us -> 25.2 us (0.74); the launches traced: 33.5 us -> 25 us
  local copies, waits for them, and re-layouts: 11.9 us -> 2.98 us
  Pallas kernels: 20.1 us -> 20.8 us
    unnamed x30 -> x4, local copies, waits for them, and re-layouts: 11.2 us -> 2.98 us
    reshape x1 -> x0, local copies, waits for them, and re-layouts: 0.69 us -> none  [fused(): norm_gain.reshape(1, -1)]
    pallas_call x1, Pallas kernels: 20.1 us -> 20.8 us  [fused(): pl.pallas_call(fused_kernel, out_shape=(jax.ShapeDtypeStruct(pair_block.s...]
where the time goes in v2:
time: 25.2 us; the launch traced here: 25 us
  Pallas kernels  20.8 us (83%)
  local copies, waits for them, and re-layouts  2.98 us (12%)
  between operations  1.3 us (5%)
    pallas_call x1, Pallas kernels, fused(): pl.pallas_call(fused_kernel, out_shape=(jax.ShapeDtypeStruct(pair_block.s...  20.8 us
    unnamed x4, local copies, waits for them, and re-layouts  2.98 us

profile of v2, /device:TPU:0, one launch (start us, length us, event | category | flops | bytes accessed | tf_op | source)
XLA Modules:
  0.0 25.0 jit_solution(6766079859949215013)
XLA Ops:
  1.3 20.8 %shard_map.185 = (f32[2,8,144,128]{3,2,1,0:T(8,128)}, bf16[2,8,768]{2,1,0:T(8,128)(2,1)}) custom-call(s32[2,8]{1,0:T(2,128)} %query_chain.1, s32[1]{0:T(128)S(6)} %copy.22.timestep, bf16[50,768]{1,0:T(8,128)(2,1)} %operands_results_scratch_0_.1, bf16[2,8,768]{2,1,0:T(8,128)(2,1)} %operands_results_scratch_1_.1, s32[2,8]{1,0:T(2,128)} %operands_results_scratch_2_.1, ...), custom_call_target="tpu_custom_call" | custom-call | tf_op jit(solution)/shard_map/pallas_call | solution.py:458
  22.1 0.0 copy-start
  22.1 2.4 %copy.23 = f32[2,8,144,128]{3,2,1,0:T(8,128)} copy(f32[2,8,144,128]{3,2,1,0:T(8,128)} %get-tuple-element.4) | data formatting | bytes 2359296
  24.4 0.0 copy-done
  24.4 0.6 %copy.24 = bf16[2,8,768]{2,1,0:T(8,128)(2,1)} copy(bf16[2,8,768]{2,1,0:T(8,128)(2,1)S(1)} %copy-done) | data formatting | bytes 49152
Async XLA Ops:
  22.1 2.4 %copy-start = (bf16[2,8,768]{2,1,0:T(8,128)(2,1)S(1)}, bf16[2,8,768]{2,1,0:T(8,128)(2,1)}, u32[]{:S(2)}) copy-start(bf16[2,8,768]{2,1,0:T(8,128)(2,1)} %get-tuple-element.5) | copy-start | bytes 73732

commit v3 on v2

--- a/solution.py
+++ b/solution.py
@@ -273,23 +273,27 @@
 
     for load in loads[8:14]:
         load.wait()
-    left_factor = dot_nt(query_norm, left_proj[...])
-    right_factor = dot_nt(key_norm, right_proj[...])
     square = rank * rank
-    spread_left = (iota((rank, square), 1) // rank == iota((rank, square), 0)).astype(jnp.float32)
-    left_wide = dot_nn(left_factor, spread_left, HIGHEST)
+    terms = 6
+    spread_left = iota((square, rank), 0) // rank == iota((square, rank), 1)
+    left_spread = dot_nn(spread_left.astype(jnp.bfloat16), left_proj[...]).astype(jnp.bfloat16)
+    tile_right = iota((terms * rank, rank), 0) % rank == iota((terms * rank, rank), 1)
+    right_tiled = dot_nn(tile_right.astype(jnp.bfloat16), right_proj[...]).astype(jnp.bfloat16)
+    left_wide = dot_nt(query_norm, left_spread)
+    right_wide = dot_nt(key_norm, right_tiled)
     on_rank = iota((rows, rank, square), 2) % rank == iota((rows, rank, square), 1)
     left_blocks = jnp.where(on_rank, left_wide[:, None, :], 0.0).reshape(rows * rank, square)
-    mixer = dot_nn(left_blocks, outer_proj[...].astype(jnp.float32), HIGHEST)
+    left_1 = rounded(left_blocks)
+    left_2 = rounded(left_blocks - left_1)
+    left_3 = left_blocks - left_1 - left_2
+    mixer = dot_nn(
+        jnp.concatenate([left_1, left_2, left_3], axis=1).astype(jnp.bfloat16),
+        jnp.concatenate([outer_proj[...]] * 3, axis=0),
+    )
     mixer = jnp.concatenate(
         [mixer[row * rank : (row + 1) * rank] for row in range(rows)], axis=1
     )
 
-    terms = 6
-    tile_right = (iota((rank, terms * rank), 1) % rank == iota((rank, terms * rank), 0)).astype(
-        jnp.float32
-    )
-    right_wide = dot_nn(right_factor, tile_right, HIGHEST)
     right_1 = rounded(right_wide)
     right_2 = rounded(right_wide - right_1)
     right_3 = right_wide - right_1 - right_2
@@ -346,9 +350,11 @@
     )
     for place in range(cols):
         gates[place] = gate[place * own_rows : (place + 1) * own_rows]
-    on_head = iota((rows, slots, width), 2) // head_width == iota((rows, slots, width), 1)
+    on_head = (
+        iota((1, slots, width), 2) // head_width == iota((1, slots, width), 1)
+    ).astype(jnp.float32)
     query_blocks = (
-        jnp.where(on_head, query[:, None, :], 0.0)
+        (on_head * query[:, None, :])
         .reshape(rows * slots, width)
         .astype(jnp.bfloat16)
     )
@@ -360,11 +366,11 @@
     exponent = jnp.exp(scores - maxima)
     totals = jnp.sum(exponent, axis=1, keepdims=True)
     summed = dot_nn(exponent.astype(jnp.bfloat16), keys_values[1]).reshape(rows, slots, width)
-    summed = jnp.sum(jnp.where(on_head, summed, 0.0), axis=1)
-    on_lane = iota((rows, slots, LANES), 2) == iota((rows, slots, LANES), 1)
+    summed = jnp.sum(on_head * summed, axis=1)
+    on_lane = (iota((1, slots, LANES), 2) == iota((1, slots, LANES), 1)).astype(jnp.float32)
 
     def by_lane(column):
-        return jnp.sum(jnp.where(on_lane, column.reshape(rows, slots, 1), 0.0), axis=1)
+        return jnp.sum(on_lane * column.reshape(rows, slots, 1), axis=1)
 
     bundle = jnp.concatenate([summed, by_lane(maxima), by_lane(totals)], axis=1)
     for place in range(cols):
@@ -382,9 +388,8 @@
     partial[me] = packed[me]
     gate_own = gates[me]
     spread_heads = (
-        (iota((LANES, width), 1) // head_width == iota((LANES, width), 0))
-        .astype(jnp.float32)
-    )
+        iota((2 * LANES, width), 1) // head_width == iota((2 * LANES, width), 0) % LANES
+    ).astype(jnp.bfloat16)
     loads[15].wait()
     for copy in p_copies:
         copy.wait()
@@ -395,8 +400,10 @@
     scales = [jnp.exp(part - peak) for part in maxima]
     total = functools.reduce(jnp.add, [a * b for a, b in zip(totals, scales)])
     total = jnp.where(iota(total.shape, 1) < heads, total, 1.0)
+    share = jnp.concatenate([scale / total for scale in scales], axis=0)
+    upper = rounded(share)
     shares = dot_nn(
-        jnp.concatenate([scale / total for scale in scales], axis=0), spread_heads, HIGHEST
+        jnp.concatenate([upper, share - upper], axis=1).astype(jnp.bfloat16), spread_heads
     )
     joint = functools.reduce(
         jnp.add,
@@ -433,6 +440,23 @@
 
 LANES = 128
 OPERANDS = 16
+VMEM_BYTES = 60 * 1024 * 1024
+
+
+def hand_on(pair_in, update_in, pair_out, update_out, pair_sem, update_sem):
+    slabs, slab_rows = pair_in.shape[:2]
+    copies = [pltpu.make_async_copy(update_in, update_out, update_sem)]
+    for slab in range(slabs):
+        for row in range(slab_rows):
+            copies.append(
+                pltpu.make_async_copy(
+                    pair_in.at[slab, row], pair_out.at[slab, row], pair_sem.at[slab, row]
+                )
+            )
+    for copy in copies:
+        copy.start()
+    for copy in copies:
+        copy.wait()
 
 
 def fused(
@@ -455,7 +479,7 @@
     smem = pl.BlockSpec(memory_space=pltpu.SMEM)
     far = pl.BlockSpec(memory_space=pltpu.HBM)
     dma = pltpu.SemaphoreType.DMA
-    return pl.pallas_call(
+    results = pl.pallas_call(
         fused_kernel,
         out_shape=(
             jax.ShapeDtypeStruct(pair_block.shape, jnp.float32),
@@ -485,9 +509,17 @@
             dma((cols - 1,)),
         ],
         compiler_params=pltpu.CompilerParams(
-            collective_id=0, has_side_effects=True, vmem_limit_bytes=60 * 1024 * 1024
+            collective_id=0, has_side_effects=True, vmem_limit_bytes=VMEM_BYTES
         ),
     )(query_chain, timestep, *operands)
+    return pl.pallas_call(
+        hand_on,
+        out_shape=tuple(jax.ShapeDtypeStruct(part.shape, part.dtype) for part in results),
+        in_specs=[far, far],
+        out_specs=(far, far),
+        scratch_shapes=[dma((slabs, slab_rows)), dma],
+        compiler_params=pltpu.CompilerParams(vmem_limit_bytes=VMEM_BYTES),
+    )(*results)
 
 
 def serve(*arrays):

time: 25.2 us -> 59.9 us (2.38)
  Pallas kernels: 20.8 us -> 58.5 us
  local copies, waits for them, and re-layouts: 2.98 us -> 0 us
    pallas_call x0 -> x1, Pallas kernels: none -> 37.7 us  [fused(): pl.pallas_call(hand_on, out_shape=tuple((jax.ShapeDtypeStruct(part.shape,...]
    unnamed x4 -> x0, local copies, waits for them, and re-layouts: 2.98 us -> none
where the time goes in v3:
time: 59.9 us; the launch traced here: 59.8 us
  Pallas kernels  58.5 us (98%)
  between operations  1.29 us (2%)
    pallas_call x1, Pallas kernels, fused(): pl.pallas_call(hand_on, out_shape=tuple((jax.ShapeDtypeStruct(part.shape,...  37.7 us
    pallas_call x1, Pallas kernels, fused(): pl.pallas_call(fused_kernel, out_shape=(jax.ShapeDtypeStruct(pair_block.s...  20.7 us

profile of v3, /device:TPU:0, one launch (start us, length us, event | category | flops | bytes accessed | tf_op | source)
XLA Modules:
  0.0 59.8 jit_solution(12527731685297883950)
XLA Ops:
  1.3 20.7 %shard_map.185 = (f32[2,8,144,128]{3,2,1,0:T(8,128)}, bf16[2,8,768]{2,1,0:T(8,128)(2,1)}) custom-call(s32[2,8]{1,0:T(2,128)} %query_chain.1, s32[1]{0:T(128)S(6)} %copy.20.timestep, bf16[50,768]{1,0:T(8,128)(2,1)} %operands_results_scratch_0_.1, bf16[2,8,768]{2,1,0:T(8,128)(2,1)} %operands_results_scratch_1_.1, s32[2,8]{1,0:T(2,128)} %operands_results_scratch_2_.1, ...), custom_call_target="tpu_custom_call" | custom-call | tf_op jit(solution)/shard_map/pallas_call | solution.py:482
  22.0 37.7 %shard_map.186 = (f32[2,8,144,128]{3,2,1,0:T(8,128)}, bf16[2,8,768]{2,1,0:T(8,128)(2,1)}) custom-call(f32[2,8,144,128]{3,2,1,0:T(8,128)} %get-tuple-element.4.pair_in, bf16[2,8,768]{2,1,0:T(8,128)(2,1)} %get-tuple-element.5.update_in), custom_call_target="tpu_custom_call" | custom-call | tf_op jit(solution)/shard_map/pallas_call | solution.py:515

commit v4 on v3

--- a/solution.py
+++ b/solution.py
@@ -173,7 +173,7 @@
     query_chain, timestep, *operands_results_scratch
 ):
     sources = operands_results_scratch[:OPERANDS]
-    new_pair_hbm, single_update = operands_results_scratch[OPERANDS : OPERANDS + 2]
+    new_pair, single_update = operands_results_scratch[OPERANDS : OPERANDS + 2]
     targets = operands_results_scratch[OPERANDS + 2 : 2 * OPERANDS + 2]
     (
         time_table, query_single, query_mask, norm_gain, query_proj, key_single, key_mask,
@@ -181,8 +181,8 @@
         out_proj,
     ) = targets
     (
-        fresh, parts_q, keys_values, bias, packed, partial, gates, final,
-        load_sem, store_sem, q_send, q_recv, kv_send, kv_recv, p_send, p_recv, f_send, f_recv,
+        parts_q, keys_values, bias, packed, partial, gates, final,
+        load_sem, q_send, q_recv, kv_send, kv_recv, p_send, p_recv, f_send, f_recv,
     ) = operands_results_scratch[2 * OPERANDS + 2 :]
     cols = lax.axis_size("col")
     me = lax.axis_index("col")
@@ -327,15 +327,13 @@
     for row in range(rows):
         slab, place = row // slab_rows, row % slab_rows
         updated = pair[slab, place] + change[:, row * channels : (row + 1) * channels]
-        fresh[slab, place] = updated
+        new_pair[slab, place] = updated
         upper = rounded(updated)
         both = jnp.concatenate([upper, updated - upper], axis=1).astype(jnp.bfloat16)
         logits = dot_nt(bias_terms, both)
         differ = (chains != query_chain[slab, place]).astype(jnp.float32)
         bias[slab, place] = logits[:slots] + logits[slots:] + chain_column * differ
 
-    store = pltpu.make_async_copy(fresh, new_pair_hbm, store_sem)
-    store.start()
 
     for copy in q_copies:
         copy.wait()
@@ -428,7 +426,6 @@
     ]
     for copy in f_copies:
         copy.start()
-    store.wait()
     for copy in f_copies:
         copy.wait()
     single_update[...] = (
@@ -444,15 +441,11 @@
 
 
 def hand_on(pair_in, update_in, pair_out, update_out, pair_sem, update_sem):
-    slabs, slab_rows = pair_in.shape[:2]
-    copies = [pltpu.make_async_copy(update_in, update_out, update_sem)]
-    for slab in range(slabs):
-        for row in range(slab_rows):
-            copies.append(
-                pltpu.make_async_copy(
-                    pair_in.at[slab, row], pair_out.at[slab, row], pair_sem.at[slab, row]
-                )
-            )
+    slabs = pair_in.shape[0]
+    copies = [
+        pltpu.make_async_copy(pair_in.at[slab], pair_out.at[slab], pair_sem.at[slab])
+        for slab in range(slabs)
+    ] + [pltpu.make_async_copy(update_in, update_out, update_sem)]
     for copy in copies:
         copy.start()
     for copy in copies:
@@ -477,19 +470,19 @@
         bias_proj.T, chain_weight.reshape(1, -1), key_chain.reshape(1, -1), pair_block, out_proj,
     )
     smem = pl.BlockSpec(memory_space=pltpu.SMEM)
+    near = pl.BlockSpec(memory_space=pltpu.VMEM)
     far = pl.BlockSpec(memory_space=pltpu.HBM)
     dma = pltpu.SemaphoreType.DMA
     results = pl.pallas_call(
         fused_kernel,
         out_shape=(
-            jax.ShapeDtypeStruct(pair_block.shape, jnp.float32),
-            jax.ShapeDtypeStruct(query_single.shape, jnp.bfloat16),
+            pltpu.VMEM(pair_block.shape, jnp.float32),
+            pltpu.VMEM(query_single.shape, jnp.bfloat16),
         ),
         in_specs=[smem, smem] + [far] * len(operands),
-        out_specs=(far, pl.BlockSpec(memory_space=pltpu.VMEM)),
+        out_specs=(near, near),
         scratch_shapes=[pltpu.VMEM(operand.shape, operand.dtype) for operand in operands]
         + [
-            pltpu.VMEM(pair_block.shape, jnp.float32),
             pltpu.VMEM((cols, rows, query_proj.shape[1]), jnp.bfloat16),
             pltpu.VMEM((2, keys, width), jnp.bfloat16),
             pltpu.VMEM((slabs, slab_rows, slots, keys), jnp.float32),
@@ -498,7 +491,6 @@
             pltpu.VMEM((cols, own_rows, width), jnp.float32),
             pltpu.VMEM((cols, own_rows, width), jnp.float32),
             dma((len(operands),)),
-            dma,
             dma((cols - 1,)),
             dma((cols - 1,)),
             dma,
@@ -515,10 +507,10 @@
     return pl.pallas_call(
         hand_on,
         out_shape=tuple(jax.ShapeDtypeStruct(part.shape, part.dtype) for part in results),
-        in_specs=[far, far],
+        in_specs=[near, near],
         out_specs=(far, far),
-        scratch_shapes=[dma((slabs, slab_rows)), dma],
-        compiler_params=pltpu.CompilerParams(vmem_limit_bytes=VMEM_BYTES),
+        scratch_shapes=[dma((slabs,)), dma],
+        compiler_params=pltpu.CompilerParams(vmem_limit_bytes=VMEM_BYTES // 60),
     )(*results)
 
 

time: 59.9 us -> 22.6 us (0.38)
  Pallas kernels: 58.5 us -> 21.2 us
    pallas_call x1, Pallas kernels: 37.7 us -> 1.04 us  [fused(): pl.pallas_call(hand_on, out_shape=tuple((jax.ShapeDtypeStruct(part.shape,...]
    pallas_call x1, Pallas kernels: 20.7 us -> 20.1 us  [fused(): pl.pallas_call(fused_kernel, out_shape=(pltpu.VMEM(pair_block.shape, jnp....]
where the time goes in v4:
time: 22.6 us; the launch traced here: 22.5 us
  Pallas kernels  21.2 us (94%)
  between operations  1.29 us (6%)
    pallas_call x1, Pallas kernels, fused(): pl.pallas_call(fused_kernel, out_shape=(pltpu.VMEM(pair_block.shape, jnp....  20.1 us
    pallas_call x1, Pallas kernels, fused(): pl.pallas_call(hand_on, out_shape=tuple((jax.ShapeDtypeStruct(part.shape,...  1.04 us

profile of v4, /device:TPU:0, one launch (start us, length us, event | category | flops | bytes accessed | tf_op | source)
XLA Modules:
  0.0 22.5 jit_solution(1118608932725088636)
XLA Ops:
  1.3 20.1 %shard_map.185 = (f32[2,8,144,128]{3,2,1,0:T(8,128)S(1)}, bf16[2,8,768]{2,1,0:T(8,128)(2,1)S(1)}) custom-call(s32[2,8]{1,0:T(2,128)} %query_chain.1, s32[1]{0:T(128)S(6)} %copy.20.timestep, bf16[50,768]{1,0:T(8,128)(2,1)} %operands_results_scratch_0_.1, bf16[2,8,768]{2,1,0:T(8,128)(2,1)} %operands_results_scratch_1_.1, s32[2,8]{1,0:T(2,128)} %operands_results_scratch_2_.1, ...), custom_call_target="tpu_custom_call" | custom-call | tf_op jit(solution)/shard_map/pallas_call | solution.py:476
  21.4 1.0 %shard_map.186 = (f32[2,8,144,128]{3,2,1,0:T(8,128)}, bf16[2,8,768]{2,1,0:T(8,128)(2,1)}) custom-call(f32[2,8,144,128]{3,2,1,0:T(8,128)S(1)} %get-tuple-element.4.pair_in, bf16[2,8,768]{2,1,0:T(8,128)(2,1)S(1)} %get-tuple-element.5.update_in), custom_call_target="tpu_custom_call" | custom-call | tf_op jit(solution)/shard_map/pallas_call | solution.py:507

commit v5 on v4

--- a/solution.py
+++ b/solution.py
@@ -262,17 +262,9 @@
     loads[6].wait()
     key_flags = column_of(key_mask[...].astype(jnp.float32), keys)
     key_norm = normal(key_single[...].astype(jnp.float32) + key_flags * time_row)
-    loads[7].wait()
-    keys_values[side] = dot_nn(key_norm, kv_proj[...]).astype(jnp.bfloat16)
-    kv_copy = pltpu.make_async_remote_copy(
-        src_ref=keys_values.at[side], dst_ref=keys_values.at[side],
-        send_sem=kv_send, recv_sem=kv_recv,
-        device_id={"row": 1 - side}, device_id_type=pl.DeviceIdType.MESH,
-    )
-    kv_copy.start()
-
     for load in loads[8:14]:
         load.wait()
+
     square = rank * rank
     terms = 6
     spread_left = iota((square, rank), 0) // rank == iota((square, rank), 1)
@@ -280,7 +272,6 @@
     tile_right = iota((terms * rank, rank), 0) % rank == iota((terms * rank, rank), 1)
     right_tiled = dot_nn(tile_right.astype(jnp.bfloat16), right_proj[...]).astype(jnp.bfloat16)
     left_wide = dot_nt(query_norm, left_spread)
-    right_wide = dot_nt(key_norm, right_tiled)
     on_rank = iota((rows, rank, square), 2) % rank == iota((rows, rank, square), 1)
     left_blocks = jnp.where(on_rank, left_wide[:, None, :], 0.0).reshape(rows * rank, square)
     left_1 = rounded(left_blocks)
@@ -294,13 +285,6 @@
         [mixer[row * rank : (row + 1) * rank] for row in range(rows)], axis=1
     )
 
-    right_1 = rounded(right_wide)
-    right_2 = rounded(right_wide - right_1)
-    right_3 = right_wide - right_1 - right_2
-    group = iota(right_wide.shape, 1) // rank
-    right_terms = jnp.where(
-        group < 3, right_1, jnp.where(group < 5, right_2, right_3)
-    ).astype(jnp.bfloat16)
     mixer_1 = rounded(mixer)
     mixer_2 = rounded(mixer - mixer_1)
     mixer_3 = mixer - mixer_1 - mixer_2
@@ -321,6 +305,25 @@
     ).astype(jnp.bfloat16)
     chain_column = column_of(chain_weight[...], slots)
     chains = key_chain[...]
+
+
+    loads[7].wait()
+    projected = dot_nn(key_norm, kv_proj[...]).astype(jnp.bfloat16)
+    right_wide = dot_nt(key_norm, right_tiled)
+    right_1 = rounded(right_wide)
+    right_2 = rounded(right_wide - right_1)
+    right_3 = right_wide - right_1 - right_2
+    group = iota(right_wide.shape, 1) // rank
+    right_terms = jnp.where(
+        group < 3, right_1, jnp.where(group < 5, right_2, right_3)
+    ).astype(jnp.bfloat16)
+    keys_values[side] = projected
+    kv_copy = pltpu.make_async_remote_copy(
+        src_ref=keys_values.at[side], dst_ref=keys_values.at[side],
+        send_sem=kv_send, recv_sem=kv_recv,
+        device_id={"row": 1 - side}, device_id_type=pl.DeviceIdType.MESH,
+    )
+    kv_copy.start()
 
     loads[14].wait()
     change = dot_nn(right_terms, mixer_terms)

time: 22.6 us -> 22.6 us (level)
  no operation moved by 1% of the time
where the time goes in v5:
time: 22.6 us; the launch traced here: 22.5 us
  Pallas kernels  21.2 us (94%)
  between operations  1.29 us (6%)
    pallas_call x1, Pallas kernels, fused(): pl.pallas_call(fused_kernel, out_shape=(pltpu.VMEM(pair_block.shape, jnp....  20.1 us
    pallas_call x1, Pallas kernels, fused(): pl.pallas_call(hand_on, out_shape=tuple((jax.ShapeDtypeStruct(part.shape,...  1.04 us

profile of v5, /device:TPU:0, one launch (start us, length us, event | category | flops | bytes accessed | tf_op | source)
XLA Modules:
  0.0 22.5 jit_solution(3733085075221750441)
XLA Ops:
  1.3 20.1 %shard_map.185 = (f32[2,8,144,128]{3,2,1,0:T(8,128)S(1)}, bf16[2,8,768]{2,1,0:T(8,128)(2,1)S(1)}) custom-call(s32[2,8]{1,0:T(2,128)} %query_chain.1, s32[1]{0:T(128)S(6)} %copy.20.timestep, bf16[50,768]{1,0:T(8,128)(2,1)} %operands_results_scratch_0_.1, bf16[2,8,768]{2,1,0:T(8,128)(2,1)} %operands_results_scratch_1_.1, s32[2,8]{1,0:T(2,128)} %operands_results_scratch_2_.1, ...), custom_call_target="tpu_custom_call" | custom-call | tf_op jit(solution)/shard_map/pallas_call | solution.py:479
  21.4 1.0 %shard_map.186 = (f32[2,8,144,128]{3,2,1,0:T(8,128)}, bf16[2,8,768]{2,1,0:T(8,128)(2,1)}) custom-call(f32[2,8,144,128]{3,2,1,0:T(8,128)S(1)} %get-tuple-element.4.pair_in, bf16[2,8,768]{2,1,0:T(8,128)(2,1)S(1)} %get-tuple-element.5.update_in), custom_call_target="tpu_custom_call" | custom-call | tf_op jit(solution)/shard_map/pallas_call | solution.py:510

commit v6 on v5

--- a/solution.py
+++ b/solution.py
@@ -169,6 +169,31 @@
     return jnp.sum(jnp.where(spot, row, jnp.zeros_like(row)), axis=1, keepdims=True)
 
 
+class Pieces:
+    def __init__(self, source, target, sems):
+        count = source.shape[0]
+        pieces = PIECES if count % (16 * PIECES) == 0 else 1
+        if len(source.shape) == 4:
+            pieces = math.gcd(count, PIECES)
+        size = count // pieces
+        self.copies = [
+            pltpu.make_async_copy(
+                source.at[pl.ds(piece * size, size)],
+                target.at[pl.ds(piece * size, size)],
+                sems.at[piece],
+            )
+            for piece in range(pieces)
+        ]
+
+    def start(self):
+        for copy in self.copies:
+            copy.start()
+
+    def wait(self):
+        for copy in self.copies:
+            copy.wait()
+
+
 def fused_kernel(
     query_chain, timestep, *operands_results_scratch
 ):
@@ -190,7 +215,7 @@
     peers = [lax.rem(me + offset, cols) for offset in range(1, cols)]
 
     loads = [
-        pltpu.make_async_copy(source, target, load_sem.at[place])
+        Pieces(source, target, load_sem.at[place])
         for place, (source, target) in enumerate(zip(sources, targets))
     ]
     for load in loads:
@@ -440,6 +465,7 @@
 
 LANES = 128
 OPERANDS = 16
+PIECES = 4
 VMEM_BYTES = 60 * 1024 * 1024
 
 
@@ -493,7 +519,7 @@
             pltpu.VMEM((cols, own_rows, width + 2 * LANES), jnp.float32),
             pltpu.VMEM((cols, own_rows, width), jnp.float32),
             pltpu.VMEM((cols, own_rows, width), jnp.float32),
-            dma((len(operands),)),
+            dma((len(operands), PIECES)),
             dma((cols - 1,)),
             dma((cols - 1,)),
             dma,

time: 22.6 us -> 23.1 us (1.022)
  Pallas kernels: 21.2 us -> 21.6 us
    pallas_call x1, Pallas kernels: 20.1 us -> 20.6 us  [fused(): pl.pallas_call(fused_kernel, out_shape=(pltpu.VMEM(pair_block.shape, jnp....]
where the time goes in v6:
time: 23.1 us; the launch traced here: 22.9 us
  Pallas kernels  21.6 us (94%)
  between operations  1.29 us (6%)
    pallas_call x1, Pallas kernels, fused(): pl.pallas_call(fused_kernel, out_shape=(pltpu.VMEM(pair_block.shape, jnp....  20.6 us
    pallas_call x1, Pallas kernels, fused(): pl.pallas_call(hand_on, out_shape=tuple((jax.ShapeDtypeStruct(part.shape,...  1.04 us

profile of v6, /device:TPU:0, one launch (start us, length us, event | category | flops | bytes accessed | tf_op | source)
XLA Modules:
  0.0 22.9 jit_solution(10754658163156515387)
XLA Ops:
  1.3 20.6 %shard_map.185 = (f32[2,8,144,128]{3,2,1,0:T(8,128)S(1)}, bf16[2,8,768]{2,1,0:T(8,128)(2,1)S(1)}) custom-call(s32[2,8]{1,0:T(2,128)} %query_chain.1, s32[1]{0:T(128)S(6)} %copy.20.timestep, bf16[50,768]{1,0:T(8,128)(2,1)} %operands_results_scratch_0_.1, bf16[2,8,768]{2,1,0:T(8,128)(2,1)} %operands_results_scratch_1_.1, s32[2,8]{1,0:T(2,128)} %operands_results_scratch_2_.1, ...), custom_call_target="tpu_custom_call" | custom-call | tf_op jit(solution)/shard_map/pallas_call | solution.py:505
  21.9 1.0 %shard_map.186 = (f32[2,8,144,128]{3,2,1,0:T(8,128)}, bf16[2,8,768]{2,1,0:T(8,128)(2,1)}) custom-call(f32[2,8,144,128]{3,2,1,0:T(8,128)S(1)} %get-tuple-element.4.pair_in, bf16[2,8,768]{2,1,0:T(8,128)(2,1)S(1)} %get-tuple-element.5.update_in), custom_call_target="tpu_custom_call" | custom-call | tf_op jit(solution)/shard_map/pallas_call | solution.py:536
